TPU v7x, 1024 devices: a whole 4x4x32 slice. The times are simulated.
1024 devices in a mesh: dom: 64 (over x, z_lo, core), grp: 16 (over y, z_hi).
Axes of the slice: x: 4, y: 4, z: 32 (z_hi: 4, z_lo: 8; z = z_hi * 8 + z_lo), core: 2. Of those that a mesh axis runs over, the one named last changes fastest.
Arguments:
- orbitals: float32 [512, 384, 512], P('grp', 'dom'), may hold values from -10 to 10, as said below
- potential: float32 [384, 512], P('dom'), may hold values from -2 to 2
Outputs:
- filtered: float32 [512, 384, 512], P('grp', 'dom')
- correlation: float32 [512, 512], P('grp', 'dom')
Inputs may be any that keep to these rules, and one draw needn't show every extreme that they name: `orbitals`: entries of order one.
All inputs are finite; a program needn't handle non-finite values.
Results may differ from a plain program's by a relative error of at most 0.003.
Values may be sent and summed in bfloat16 or wider, within the bound.
A program may use at most 32 MiB of HBM per device.

v0:
```python
import jax
import jax.numpy as jnp
from jax import lax
from jax.sharding import PartitionSpec as P

NX = 32
NY = 16


COEFFS = [
    -5369.0 / 1800.0,
    12.0 / 7.0,
    -15.0 / 56.0,
    10.0 / 189.0,
    -1.0 / 112.0,
    2.0 / 1925.0,
    -1.0 / 16632.0,
]
CENTER = 13.0
HALF_WIDTH = 11.0


def padded_2(cells, sides, width):
    for axis, dim in sides:
        count = lax.axis_size(axis)
        head = lax.slice_in_dim(cells, 0, width, axis=dim)
        tail = lax.slice_in_dim(cells, cells.shape[dim] - width, cells.shape[dim], axis=dim)
        cells = jnp.concatenate(
            [
                lax.ppermute(tail, axis, [(i, (i + 1) % count) for i in range(count)]),
                cells,
                lax.ppermute(head, axis, [((i + 1) % count, i) for i in range(count)]),
            ],
            axis=dim,
        )
    return cells


def plane_stencil():
    cells = jnp.arange(NY * NX, dtype=jnp.int32)
    row_of = cells // NX
    col_of = cells % NX
    row_gap = (row_of[:, None] - row_of[None, :]) % NY
    col_gap = (col_of[:, None] - col_of[None, :]) % NX
    same_row = row_of[:, None] == row_of[None, :]
    same_col = col_of[:, None] == col_of[None, :]
    stencil = 2.0 * COEFFS[0] * jnp.where(same_row & same_col, 1.0, 0.0).astype(jnp.float32)
    for reach in range(1, 7):
        along_rows = same_col & ((row_gap == reach) | (row_gap == NY - reach))
        along_cols = same_row & ((col_gap == reach) | (col_gap == NX - reach))
        stencil = stencil + COEFFS[reach] * jnp.where(along_rows, 1.0, 0.0).astype(jnp.float32)
        stencil = stencil + COEFFS[reach] * jnp.where(along_cols, 1.0, 0.0).astype(jnp.float32)
    return stencil


def hamiltonian(block, field, stencil):
    count = block.shape[0]
    planes = block.shape[1]
    cells = block.shape[2]
    padded = padded_2(block, (("dom", 1),), 6)
    in_plane = jnp.dot(
        block.reshape((count * planes, cells)),
        stencil,
        precision=lax.Precision.HIGHEST,
        preferred_element_type=jnp.float32,
    ).reshape(block.shape)
    laplace = in_plane + COEFFS[0] * block
    for reach in range(1, 7):
        along_z = (
            padded[:, 6 + reach : 6 + reach + planes] + padded[:, 6 - reach : 6 - reach + planes]
        )
        laplace = laplace + COEFFS[reach] * along_z
    return -0.5 / 0.25 * laplace + field[None] * block


def shards(orbitals, potential):
    stencil = plane_stencil()
    previous = orbitals
    current = (hamiltonian(orbitals, potential, stencil) - CENTER * orbitals) / HALF_WIDTH
    for degree in range(3):
        following = (
            2.0 * (hamiltonian(current, potential, stencil) - CENTER * current) / HALF_WIDTH
            - previous
        )
        previous = current
        current = following
    own_count = current.shape[0]
    local_cells = current.shape[1] * current.shape[2]
    total_cells = local_cells * lax.axis_size("dom")
    mine = current.astype(jnp.bfloat16).reshape(own_count, local_cells)
    tile = lax.dot_general(
        mine,
        lax.all_gather(mine, "grp", axis=0, tiled=True),
        (((1,), (1,)), ((), ())),
        preferred_element_type=jnp.float32,
    )
    summed = lax.psum_scatter(tile, "dom", scatter_dimension=1, tiled=True)
    correlation = summed / total_cells
    return (current, correlation)


def solution(mesh):
    in_specs = (P("grp", "dom", None), P("dom", None))
    out_specs = (P("grp", "dom", None), P("grp", "dom"))
    return jax.shard_map(shards, mesh=mesh, in_specs=in_specs, out_specs=out_specs, check_vma=False)
```

profile of v0, /device:TPU:1, one launch (start us, length us, event | category | flops | bytes accessed | tf_op | source)
XLA Modules:
  0.0 1136.6 jit_solution(14204556781207621193)
XLA Ops:
  7.2 0.0 all-gather.2.cloned.1.call-start
  7.2 4.9 collective-permute-start.1
  12.2 13.0 %collective-permute-start = (f32[32,6,512]{2,0,1:T(8,128)}, f32[32,6,512]{2,0,1:T(8,128)S(1)}, u32[]{:S(2)}, u32[]{:S(2)}) collective-permute-start(f32[32,6,512]{2,0,1:T(8,128)} %param.2), channel_id=1, source_target_pairs={{16,0},{32,16},{48,32},{64,48},{80,64},{96,80},{112,96},{128,112},... | collective-permute-start | bytes 1179656 | tf_op jit(solution)/shard_map/ppermute | solution.py:32
  25.2 1.2 copy.8
  26.5 0.1 reshape.70
  26.5 0.0 copy-start
  26.5 5.3 convolution_bitcast_fusion
  31.9 0.0 copy-start.2
  31.9 0.1 reshape.71
  31.9 0.0 collective-permute-done.1
  32.0 0.0 copy-done
  32.0 0.1 constant_dynamic-update-slice_fusion.1
  32.1 0.0 collective-permute-done
  32.1 0.5 copy-done.2
  32.6 0.6 broadcast_multiply_fusion
  33.2 12.4 %collective-permute-start.2 = (f32[32,6,512]{2,0,1:T(8,128)S(1)}, f32[32,6,512]{2,0,1:T(8,128)S(1)}, u32[]{:S(2)}, u32[]{:S(2)}) collective-permute-start(f32[32,6,512]{2,0,1:T(8,128)S(1)} %get-tuple-element.2), channel_id=1, source_target_pairs={{16,0},{32,16},{48,32},{64,48},{80,64},{96,80},{112,96},{128,112},... | collective-permute-start | bytes 1179656 | tf_op jit(solution)/shard_map/ppermute | solution.py:32
  45.6 2.1 collective-permute-start.3
  47.7 0.0 collective-permute-done.2
  47.7 9.9 collective-permute-done.3
  57.6 5.6 fusion.69
  63.3 20.2 %collective-permute-start.4 = (f32[32,6,512]{2,0,1:T(8,128)S(1)}, f32[32,6,512]{2,0,1:T(8,128)S(1)}, u32[]{:S(2)}, u32[]{:S(2)}) collective-permute-start(f32[32,6,512]{2,0,1:T(8,128)S(1)} %fusion.69), channel_id=1, source_target_pairs={{16,0},{32,16},{48,32},{64,48},{80,64},{96,80},{112,96},{128,112},... | collective-permute-start | bytes 1179656 | tf_op jit(solution)/shard_map/ppermute | solution.py:32
  83.5 1.9 collective-permute-start.5
  85.4 0.0 collective-permute-done.4
  85.4 7.2 collective-permute-done.5
  92.6 5.6 fusion.42
  98.2 13.0 %collective-permute-start.6 = (f32[32,6,512]{2,0,1:T(8,128)S(1)}, f32[32,6,512]{2,0,1:T(8,128)S(1)}, u32[]{:S(2)}, u32[]{:S(2)}) collective-permute-start(f32[32,6,512]{2,0,1:T(8,128)S(1)} %fusion.42), channel_id=1, source_target_pairs={{16,0},{32,16},{48,32},{64,48},{80,64},{96,80},{112,96},{128,112},... | collective-permute-start | bytes 1179656 | tf_op jit(solution)/shard_map/ppermute | solution.py:32
  111.2 2.1 collective-permute-start.7
  113.3 0.0 collective-permute-done.6
  113.3 6.9 collective-permute-done.7
  120.3 5.6 fusion.15
  125.9 0.0 copy-start.1
  125.9 0.8 copy.11
  126.7 0.0 all-gather.2.cloned.1.call-update
  126.7 0.0 all-reduce.3.cloned.1.call-start
  126.7 203.6 %all-gather.2.cloned.1.call-done = bf16[512,3072]{1,0:T(8,128)(2,1)} async-done(((bf16[32,3072]{1,0:T(8,128)(2,1)}), bf16[512,3072]{1,0:T(8,128)(2,1)}) %all-gather.2.cloned.1.call-update) | async-done | bytes 3145744 | tf_op jit(solution)/shard_map/all_gather | solution.py:93
  330.4 3.7 fusion.240
  334.1 0.0 all-reduce.3.cloned.1.call-update
  334.1 1.3 dynamic-slice
  336.0 792.5 %all-reduce.3.cloned.1.call-done = f32[32,512]{0,1:T(8,128)} async-done(((f32[32,512]{0,1:T(8,128)}), f32[32,512]{0,1:T(8,128)}) %all-reduce.3.cloned.1.call-update) | async-done | bytes 65552
  1128.5 1.3 dynamic-slice_multiply_fusion
  1129.8 0.0 copy-done.1
  (5 shorter events, 0.1 us)
Async XLA Ops:
  7.2 323.2 %all-gather.2.cloned.1.call-start = ((), (), s32[]{:S(2)}) async-start(), calls=%async_computation | async-start | bytes 3342336 | tf_op jit(solution)/shard_map/all_gather | solution.py:93
  7.2 24.7 %collective-permute-start.1 = (f32[32,6,512]{2,0,1:T(8,128)}, f32[32,6,512]{2,0,1:T(8,128)S(1)}, u32[]{:S(2)}, u32[]{:S(2)}) collective-permute-start(f32[32,6,512]{2,0,1:T(8,128)} %param.2), channel_id=1, source_target_pairs={{0,16},{16,32},{32,48},{48,64},{64,80},{80,96},{96,112},{112,128},... | collective-permute-start | bytes 1179656 | tf_op jit(solution)/shard_map/ppermute | solution.py:30
  12.2 19.9 %collective-permute-start = (f32[32,6,512]{2,0,1:T(8,128)}, f32[32,6,512]{2,0,1:T(8,128)S(1)}, u32[]{:S(2)}, u32[]{:S(2)}) collective-permute-start(f32[32,6,512]{2,0,1:T(8,128)} %param.2), channel_id=1, source_target_pairs={{16,0},{32,16},{48,32},{64,48},{80,64},{96,80},{112,96},{128,112},... | collective-permute-start | bytes 1179656 | tf_op jit(solution)/shard_map/ppermute | solution.py:32
  26.5 5.4 copy-start
  31.9 0.7 copy-start.2
  33.2 14.5 %collective-permute-start.2 = (f32[32,6,512]{2,0,1:T(8,128)S(1)}, f32[32,6,512]{2,0,1:T(8,128)S(1)}, u32[]{:S(2)}, u32[]{:S(2)}) collective-permute-start(f32[32,6,512]{2,0,1:T(8,128)S(1)} %get-tuple-element.2), channel_id=1, source_target_pairs={{16,0},{32,16},{48,32},{64,48},{80,64},{96,80},{112,96},{128,112},... | collective-permute-start | bytes 1179656 | tf_op jit(solution)/shard_map/ppermute | solution.py:32
  45.6 12.1 %collective-permute-start.3 = (f32[32,6,512]{2,0,1:T(8,128)S(1)}, f32[32,6,512]{2,0,1:T(8,128)S(1)}, u32[]{:S(2)}, u32[]{:S(2)}) collective-permute-start(f32[32,6,512]{2,0,1:T(8,128)S(1)} %get-tuple-element.2), channel_id=1, source_target_pairs={{0,16},{16,32},{32,48},{48,64},{64,80},{80,96},{96,112},{112,128},... | collective-permute-start | bytes 1179656 | tf_op jit(solution)/shard_map/ppermute | solution.py:30
  63.3 22.1 %collective-permute-start.4 = (f32[32,6,512]{2,0,1:T(8,128)S(1)}, f32[32,6,512]{2,0,1:T(8,128)S(1)}, u32[]{:S(2)}, u32[]{:S(2)}) collective-permute-start(f32[32,6,512]{2,0,1:T(8,128)S(1)} %fusion.69), channel_id=1, source_target_pairs={{16,0},{32,16},{48,32},{64,48},{80,64},{96,80},{112,96},{128,112},... | collective-permute-start | bytes 1179656 | tf_op jit(solution)/shard_map/ppermute | solution.py:32
  83.5 9.1 collective-permute-start.5
  98.2 15.2 %collective-permute-start.6 = (f32[32,6,512]{2,0,1:T(8,128)S(1)}, f32[32,6,512]{2,0,1:T(8,128)S(1)}, u32[]{:S(2)}, u32[]{:S(2)}) collective-permute-start(f32[32,6,512]{2,0,1:T(8,128)S(1)} %fusion.42), channel_id=1, source_target_pairs={{16,0},{32,16},{48,32},{64,48},{80,64},{96,80},{112,96},{128,112},... | collective-permute-start | bytes 1179656 | tf_op jit(solution)/shard_map/ppermute | solution.py:32
  111.2 9.1 collective-permute-start.7
  125.9 1003.9 %copy-start.1 = (f32[32,6,512]{2,0,1:T(8,128)}, f32[32,6,512]{2,0,1:T(8,128)S(1)}, u32[]{:S(2)}) copy-start(f32[32,6,512]{2,0,1:T(8,128)S(1)} %fusion.15) | copy-start | bytes 1179652
  126.7 1001.8 %all-reduce.3.cloned.1.call-start = ((), (), s32[]{:S(2)}) async-start(), calls=%async_computation.1 | async-start | bytes 524288
Sparse Core Ops, SparseCore 0:
  126.8 203.5 all-gather.1
  334.2 794.2 all-reduce.2
where the time goes:
time: 1140 us
  waiting for transfers between devices  1020 us (89%)
  starting transfers between devices  69.8 us (6%)
  matrix products  25.8 us (2%)
  between operations  14.9 us (1%)
    unnamed x3, waiting for transfers between devices  793 us
    all_gather x1, waiting for transfers between devices, shards(): lax.all_gather(mine, 'grp', axis=0, tiled=True)  204 us
    ppermute x4, starting transfers between devices, padded_2(): lax.ppermute(head, axis, [((i + 1) % count, i) for i in range(count)])  58.6 us
    ppermute x4, waiting for transfers between devices, padded_2(): lax.ppermute(tail, axis, [(i, (i + 1) % count) for i in range(count)])  24.1 us
  transfers between devices with their start and end apart: 10, of which 5 were waited for; matrix products, arithmetic and copies ran while one was open for 1% of the time, Pallas kernels for 0%

commit v1 on v0

v1 whole, which is shorter than its diff:
```python
import jax
import jax.numpy as jnp
import ml_dtypes
import numpy as np
from jax import lax
from jax.experimental import pallas as pl
from jax.experimental.pallas import tpu as pltpu
from jax.sharding import PartitionSpec as P

NX = 32
NY = 16
CELLS = NX * NY
NZ = 384
CORES = 2
CHUNKS = 2
ROWS = 16
LANES = 128
PLANES = 6

COEFFS = [
    -5369.0 / 1800.0,
    12.0 / 7.0,
    -15.0 / 56.0,
    10.0 / 189.0,
    -1.0 / 112.0,
    2.0 / 1925.0,
    -1.0 / 16632.0,
]
CENTER = 13.0
HALF_WIDTH = 11.0
KINETIC = -0.5 / 0.25

HIGH_AT = [1, 2, 3, 4, 5, 6]
LOW_AT = [0, 8, 9, 10, 11, 7]


def plane_stencil():
    cells = np.arange(CELLS)
    row_of, col_of = cells // NX, cells % NX
    row_gap = (row_of[:, None] - row_of[None, :]) % NY
    col_gap = (col_of[:, None] - col_of[None, :]) % NX
    stencil = np.zeros((CELLS, CELLS), np.float64)
    for reach in range(1, 7):
        rows = (col_gap == 0) & ((row_gap == reach) | (row_gap == NY - reach))
        cols = (row_gap == 0) & ((col_gap == reach) | (col_gap == NX - reach))
        stencil += COEFFS[reach] / COEFFS[1] * (rows.astype(np.float64) + cols.astype(np.float64))
    return stencil.astype(ml_dtypes.bfloat16)


def make_kernel(xs, zls, ys, zhs):
    doms = xs * zls * CORES

    def kernel(
        v_hbm, pot_hbm, sten_hbm, out_hbm, corr_ref,
        buf_a, buf_b, sten, pot, diag, sbuf, from_left, from_right,
        rounded, relay, gathered, parts, got_x, sum_x, got_zl, sum_zl, got_zh,
        load_sem, store_sem, halo_send, halo_recv, z_send, z_recv, relay_recv, relay_send,
        y_send, y_recv, x_send, x_recv, zl_send, zl_recv, zh_send, zh_recv,
    ):
        dom = lax.axis_index("dom")
        grp = lax.axis_index("grp")
        core = lax.rem(dom, CORES)
        zl = lax.rem(dom // CORES, zls)
        x = dom // (CORES * zls)
        zh = lax.rem(grp, zhs)
        y = grp // zhs

        def at(x_=x, zl_=zl, core_=core, y_=y, zh_=zh):
            return {"dom": (x_ * zls + zl_) * CORES + core_, "grp": y_ * zhs + zh_}

        def shift(value, by, count):
            return lax.rem(value + (by + count), count)

        def send(src, dst, send_sem, recv_sem, device):
            copy = pltpu.make_async_remote_copy(
                src_ref=src, dst_ref=dst, send_sem=send_sem, recv_sem=recv_sem,
                device_id=device, device_id_type=pl.DeviceIdType.MESH,
            )
            copy.start()
            return copy

        left = {"dom": shift(dom, -1, doms), "grp": grp}
        right = {"dom": shift(dom, 1, doms), "grp": grp}
        x_peers = [(o, c) for o in range(xs) for c in range(CORES) if (o, c) != (0, 0)]

        def x_peer(off, flip):
            return at(x_=shift(x, off, xs), core_=lax.rem(core + flip, CORES))

        loads = []
        for c in range(CHUNKS):
            copy = pltpu.make_async_copy(
                v_hbm.at[:, pl.ds(c * ROWS, ROWS), :], buf_a.at[c], load_sem.at[c]
            )
            copy.start()
            loads.append(copy)
        pot_load = pltpu.make_async_copy(pot_hbm, pot, load_sem.at[2])
        pot_load.start()
        sten_load = pltpu.make_async_copy(sten_hbm, sten, load_sem.at[3])
        sten_load.start()

        barrier = pltpu.get_barrier_semaphore()
        peers = [left, right]
        peers += [at(zh_=shift(zh, o, zhs)) for o in range(1, zhs)]
        peers += [at(y_=shift(y, o, ys)) for o in range(1, ys)]
        peers += [x_peer(o, c) for o, c in x_peers]
        peers += [at(zl_=shift(zl, o, zls)) for o in range(1, zls)]
        for peer in peers:
            pl.semaphore_signal(barrier, inc=1, device_id=peer, device_id_type=pl.DeviceIdType.MESH)

        bufs = [buf_a, buf_b]

        def split_store(s, c, plane, lanes, value):
            high = value.astype(jnp.bfloat16)
            low = (value - high.astype(jnp.float32)).astype(jnp.bfloat16)
            sbuf[s, c, HIGH_AT[plane], :, lanes] = high
            sbuf[s, c, LOW_AT[plane], :, lanes] = low

        def local_part(s, c):
            cur, nxt = bufs[s % 2], bufs[(s + 1) % 2]
            scale = (1.0 if s == 0 else 2.0) / HALF_WIDTH
            couple = [scale * KINETIC * k for k in COEFFS]
            lhs = sbuf[s, c].reshape(12 * ROWS, CELLS)
            for half in range(2):
                wide = pl.ds(half * 256, 256)
                res = jnp.dot(lhs, sten[:, wide], preferred_element_type=jnp.float32)
                res = res.reshape(12, ROWS, 256)
                for part in range(2):
                    lanes = pl.ds(half * 256 + part * LANES, LANES)
                    own = [cur[c, p, :, lanes] for p in range(PLANES)]
                    for p in range(PLANES):
                        flat = (res[HIGH_AT[p]] + res[LOW_AT[p]])[:, part * LANES : (part + 1) * LANES]
                        total = couple[1] * flat + (scale * diag[pl.ds(p, 1), lanes]) * own[p]
                        for k in range(1, PLANES):
                            if p - k >= 0 and p + k < PLANES:
                                total += couple[k] * (own[p - k] + own[p + k])
                            elif p - k >= 0:
                                total += couple[k] * own[p - k]
                            elif p + k < PLANES:
                                total += couple[k] * own[p + k]
                        if s > 0:
                            total -= nxt[c, p, :, lanes]
                        nxt[c, p, :, lanes] = total

        def finish(s, c, lanes):
            nxt = bufs[(s + 1) % 2]
            scale = (1.0 if s == 0 else 2.0) / HALF_WIDTH
            couple = [scale * KINETIC * k for k in COEFFS]
            lower = [from_left[s, c, i, :, lanes].astype(jnp.float32) for i in range(7)]
            lower[5] = lower[5] + lower[6]
            upper = [from_right[s, c, i, :, lanes].astype(jnp.float32) for i in range(7)]
            upper = [upper[1] + upper[0]] + upper[2:]
            results = []
            for p in range(PLANES):
                total = nxt[c, p, :, lanes]
                for i in range(p, PLANES):
                    total += couple[p + 6 - i] * lower[i]
                for i in range(p + 1):
                    total += couple[6 + i - p] * upper[i]
                nxt[c, p, :, lanes] = total
                results.append(total)
            return results

        def send_halo(s, c):
            return [
                send(sbuf.at[s, c, pl.ds(0, 7)], from_right.at[s, c], halo_send.at[s, c, 0], halo_recv.at[s, c, 0], left),
                send(sbuf.at[s, c, pl.ds(1, 7)], from_left.at[s, c], halo_send.at[s, c, 1], halo_recv.at[s, c, 1], right),
            ]

        for c in range(CHUNKS):
            loads[c].wait()
            for q in range(CELLS // LANES):
                lanes = pl.ds(q * LANES, LANES)
                for p in range(PLANES):
                    split_store(0, c, p, lanes, buf_a[c, p, :, lanes])
        pot_load.wait()
        diag[...] = pot[...] + (3.0 * KINETIC * COEFFS[0] - CENTER)
        sten_load.wait()
        local_part(0, 0)
        pl.semaphore_wait(barrier, len(peers))
        halos = {}
        for c in range(CHUNKS):
            halos[0, c] = send_halo(0, c)
        for c in range(1, CHUNKS):
            local_part(0, c)

        zh_up, zh_down, zh_far = shift(zh, 1, zhs), shift(zh, -1, zhs), shift(zh, 2, zhs)
        sends = []
        stores = []
        arrivals = {}
        relays = {}
        y_arrivals = []

        def spread_y(c, rel, source):
            for o in range(1, ys):
                copy = send(
                    gathered.at[y, source, c], gathered.at[y, source, c],
                    y_send.at[c, rel, o - 1], y_recv.at[c, rel, o - 1], at(y_=shift(y, o, ys)),
                )
                sends.append(copy)
                y_arrivals.append(copy)

        for s in range(4):
            last = s == 3
            for c in range(CHUNKS):
                for copy in halos[s, c]:
                    copy.wait_recv()
                for q in range(CELLS // LANES):
                    lanes = pl.ds(q * LANES, LANES)
                    results = finish(s, c, lanes)
                    for p, value in enumerate(results):
                        if last:
                            rounded[c, q, p // 2, :, pl.ds((p % 2) * LANES, LANES)] = value.astype(jnp.bfloat16)
                        else:
                            split_store(s + 1, c, p, lanes, value)
                if not last:
                    halos[s + 1, c] = send_halo(s + 1, c)
                    local_part(s + 1, c)
                    continue
                first, other = (zh_up, zh_down) if c == 0 else (zh_down, zh_up)
                relays[c] = send(rounded.at[c, zh_far], relay.at[c], z_send.at[c, 2], relay_recv.at[c], at(zh_=first))
                arrivals[c, 0] = send(rounded.at[c, first], gathered.at[y, zh, c], z_send.at[c, 0], z_recv.at[c, 0], at(zh_=first))
                arrivals[c, 1] = send(rounded.at[c, other], gathered.at[y, zh, c], z_send.at[c, 1], z_recv.at[c, 1], at(zh_=other))
                gathered[y, zh, c] = rounded[c, zh]
                spread_y(c, 0, zh)
                copy = pltpu.make_async_copy(
                    buf_a.at[c], out_hbm.at[:, pl.ds(c * ROWS, ROWS), :], store_sem.at[c]
                )
                copy.start()
                stores.append(copy)

        for c in range(CHUNKS):
            first, other = (zh_up, zh_down) if c == 0 else (zh_down, zh_up)
            relays[c].wait_recv()
            arrivals[c, 2] = send(relay.at[c], gathered.at[y, other, c], relay_send.at[c], z_recv.at[c, 2], at(zh_=first))
            arrivals[c, 0].wait_recv()
            spread_y(c, 1, other)
            arrivals[c, 1].wait_recv()
            spread_y(c, 2, first)
        for c in range(CHUNKS):
            arrivals[c, 2].wait_recv()
            spread_y(c, 3, zh_far)
        for copy in y_arrivals:
            copy.wait_recv()

        own_rows = zhs * CHUNKS * ROWS
        x_arrivals = []
        for off in (2, 1, 3, 0):
            dest = shift(x, off, xs)
            total = jnp.zeros((own_rows, own_rows), jnp.float32)
            for i in range(PLANES // 2):
                total += lax.dot_general(
                    gathered[dest, :, :, i].reshape(own_rows, 2 * LANES),
                    gathered[y, :, :, i].reshape(own_rows, 2 * LANES),
                    (((1,), (1,)), ((), ())),
                    preferred_element_type=jnp.float32,
                )
            total = total.reshape(zls, CORES, 8, own_rows)
            for b in range(CORES):
                parts[off, b] = total[:, b]
            for flip in range(CORES):
                if (off, flip) == (0, 0):
                    continue
                copy = send(
                    parts.at[off, lax.rem(core + flip, CORES)], got_x.at[off, flip],
                    x_send.at[off, flip], x_recv.at[off, flip], x_peer(off, flip),
                )
                sends.append(copy)
                x_arrivals.append((off, flip, copy))
        total = parts[0, core]
        for off, flip, copy in x_arrivals:
            copy.wait_recv()
            total += got_x[off, flip]
        sum_x[...] = total

        zl_arrivals = []
        for o in range(1, zls):
            dest = shift(zl, o, zls)
            copy = send(sum_x.at[dest], got_zl.at[o], zl_send.at[o], zl_recv.at[o], at(zl_=dest))
            sends.append(copy)
            zl_arrivals.append(copy)
        total = sum_x[zl]
        for o, copy in enumerate(zl_arrivals):
            copy.wait_recv()
            total += got_zl[o + 1]
        sum_zl[...] = total

        zh_arrivals = []
        for o in range(1, zhs):
            dest = shift(zh, o, zhs)
            copy = send(sum_zl, got_zh.at[o], zh_send.at[o], zh_recv.at[o], at(zh_=dest))
            sends.append(copy)
            zh_arrivals.append(copy)
        for o, copy in enumerate(zh_arrivals):
            copy.wait_recv()
            total += got_zh[o + 1]
        width = CHUNKS * ROWS
        mine = jnp.zeros((8, width), jnp.float32)
        for o in range(zhs):
            mine = jnp.where(zh == o, total[:, o * width : (o + 1) * width], mine)
        corr_ref[...] = mine * (1.0 / (NZ * CELLS))

        for s in range(4):
            for c in range(CHUNKS):
                for copy in halos[s, c]:
                    copy.wait_send()
        for copy in list(relays.values()) + list(arrivals.values()) + sends:
            copy.wait_send()
        for copy in stores:
            copy.wait()

    return kernel


def solution(mesh):
    zls, zhs = 8, 4
    xs = mesh.shape["dom"] // (zls * CORES)
    ys = mesh.shape["grp"] // zhs
    stencil = plane_stencil()

    def shards(orbitals, potential):
        planes = jnp.transpose(orbitals, (1, 0, 2))
        count = planes.shape[1]
        dma = pltpu.SemaphoreType.DMA
        f32, bf16 = jnp.float32, jnp.bfloat16
        filtered, corr = pl.pallas_call(
            make_kernel(xs, zls, ys, zhs),
            out_shape=(
                jax.ShapeDtypeStruct((PLANES, count, CELLS), f32),
                jax.ShapeDtypeStruct((8, count), f32),
            ),
            in_specs=[pl.BlockSpec(memory_space=pl.ANY)] * 3,
            out_specs=(
                pl.BlockSpec(memory_space=pl.ANY),
                pl.BlockSpec(memory_space=pltpu.VMEM),
            ),
            scratch_shapes=[
                pltpu.VMEM((CHUNKS, PLANES, ROWS, CELLS), f32),
                pltpu.VMEM((CHUNKS, PLANES, ROWS, CELLS), f32),
                pltpu.VMEM((CELLS, CELLS), bf16),
                pltpu.VMEM((PLANES, CELLS), f32),
                pltpu.VMEM((PLANES, CELLS), f32),
                pltpu.VMEM((4, CHUNKS, 12, ROWS, CELLS), bf16),
                pltpu.VMEM((4, CHUNKS, 7, ROWS, CELLS), bf16),
                pltpu.VMEM((4, CHUNKS, 7, ROWS, CELLS), bf16),
                pltpu.VMEM((CHUNKS, zhs, 3, ROWS, 2 * LANES), bf16),
                pltpu.VMEM((CHUNKS, 3, ROWS, 2 * LANES), bf16),
                pltpu.VMEM((ys, zhs, CHUNKS, 3, ROWS, 2 * LANES), bf16),
                pltpu.VMEM((xs, CORES, zls, 8, LANES), f32),
                pltpu.VMEM((xs, CORES, zls, 8, LANES), f32),
                pltpu.VMEM((zls, 8, LANES), f32),
                pltpu.VMEM((zls, 8, LANES), f32),
                pltpu.VMEM((8, LANES), f32),
                pltpu.VMEM((zhs, 8, LANES), f32),
                dma((4,)),
                dma((CHUNKS,)),
                dma((4, CHUNKS, 2)),
                dma((4, CHUNKS, 2)),
                dma((CHUNKS, 3)),
                dma((CHUNKS, 3)),
                dma((CHUNKS,)),
                dma((CHUNKS,)),
                dma((CHUNKS, 4, 3)),
                dma((CHUNKS, 4, 3)),
                dma((xs, CORES)),
                dma((xs, CORES)),
                dma((zls,)),
                dma((zls,)),
                dma((zhs,)),
                dma((zhs,)),
            ],
            compiler_params=pltpu.CompilerParams(
                collective_id=0, has_side_effects=True, vmem_limit_bytes=40 * 1024 * 1024
            ),
            cost_estimate=pl.CostEstimate(flops=10**9, bytes_accessed=1500000, transcendentals=0),
        )(planes, potential, jnp.asarray(stencil))
        return jnp.transpose(filtered, (1, 0, 2)), jnp.transpose(corr, (1, 0))

    in_specs = (P("grp", "dom", None), P("dom", None))
    out_specs = (P("grp", "dom", None), P("grp", "dom"))
    return jax.shard_map(shards, mesh=mesh, in_specs=in_specs, out_specs=out_specs, check_vma=False)
```

time: 1140 us -> 123 us (0.11)
  waiting for transfers between devices: 1020 us -> 0 us
  Pallas kernels: 0 us -> 118 us
  starting transfers between devices: 69.8 us -> 0 us
  matrix products: 25.8 us -> 0 us
  between operations: 14.9 us -> 0.65 us
    unnamed x3 -> x0, waiting for transfers between devices: 793 us -> none
    all_gather x1 -> x0, waiting for transfers between devices: 204 us -> none  [shards(): lax.all_gather(mine, 'grp', axis=0, tiled=True)]
    pallas_call x0 -> x1, Pallas kernels: none -> 118 us  [shards(): pl.pallas_call(make_kernel(xs, zls, ys, zhs), out_shape=(jax.ShapeDtypeSt...]
    ppermute x8 -> x0, starting transfers between devices: 69.7 us -> none  [the longest x4 58.6 us: padded_2(): lax.ppermute(head, axis, [((i + 1) % count, i) for i in range(count)])]
    dot_general x5 -> x0, matrix products: 25.8 us -> none  [the longest x4 22.1 us: hamiltonian(): jnp.dot(block.reshape((count * planes, cells)), stencil, precision=lax.Pr...]
    ppermute x8 -> x0, waiting for transfers between devices: 24.1 us -> none  [the longest x4 24.1 us: padded_2(): lax.ppermute(tail, axis, [(i, (i + 1) % count) for i in range(count)])]
  transfers between devices with their start and end apart: 10 -> 0, of which waited for: 5 -> 0; matrix products, arithmetic and copies ran while one was open for 1% -> 0% of each run, Pallas kernels for 0% -> 0%
where the time goes in v1:
time: 123 us; the launch traced here: 122 us
  Pallas kernels  118 us (96%)
  local copies, waits for them, and re-layouts  4.09 us (3%)
    pallas_call x1, Pallas kernels, shards(): pl.pallas_call(make_kernel(xs, zls, ys, zhs), out_shape=(jax.ShapeDtypeSt...  118 us
    unnamed x8, local copies, waits for them, and re-layouts  4.09 us

profile of v1, /device:TPU:1, one launch (start us, length us, event | category | flops | bytes accessed | tf_op | source)
XLA Modules:
  0.0 122.3 jit_solution(3766740687193187664)
XLA Ops:
  0.6 0.0 copy-start
  0.6 1.0 copy-done
  1.6 0.0 copy-start.1
  1.6 0.7 copy-done.1
  2.3 0.0 copy-start.2
  2.3 1.0 copy-done.2
  3.4 117.6 %shard_map.50 = (f32[6,32,512]{2,1,0:T(8,128)S(1)}, f32[8,32]{1,0:T(8,128)S(1)}) custom-call(f32[6,32,512]{2,1,0:T(8,128)S(1)} %bitcast.5, f32[6,512]{1,0:T(8,128)S(1)} %copy-done.1, bf16[512,512]{1,0:T(8,128)(2,1)S(1)} %copy-done.2), custom_call_target="tpu_custom_call" | custom-call | flops 1000000000 | bytes 1500000 | tf_op jit(solution)/shard_map/pallas_call | solution.py:325
  121.0 0.7 copy.7
  121.7 0.6 copy.8
Async XLA Ops:
  0.6 1.0 copy-start
  1.6 0.7 copy-start.1
  2.3 1.0 copy-start.2

commit v2 on v1

--- a/solution.py
+++ b/solution.py
@@ -16,6 +16,9 @@
 ROWS = 16
 LANES = 128
 PLANES = 6
+PIECES = 2
+PIECE = CELLS // PIECES
+ROUNDS = 7
 
 COEFFS = [
     -5369.0 / 1800.0,
@@ -54,7 +57,7 @@
         v_hbm, pot_hbm, sten_hbm, out_hbm, corr_ref,
         buf_a, buf_b, sten, pot, diag, sbuf, from_left, from_right,
         rounded, relay, gathered, parts, got_x, sum_x, got_zl, sum_zl, got_zh,
-        load_sem, store_sem, halo_send, halo_recv, z_send, z_recv, relay_recv, relay_send,
+        load_sem, store_sem, token_up, token_down, halo_send, halo_recv, z_send, z_recv, relay_recv, relay_send,
         y_send, y_recv, x_send, x_recv, zl_send, zl_recv, zh_send, zh_recv,
     ):
         dom = lax.axis_index("dom")
@@ -99,13 +102,26 @@
         sten_load.start()
 
         barrier = pltpu.get_barrier_semaphore()
-        peers = [left, right]
-        peers += [at(zh_=shift(zh, o, zhs)) for o in range(1, zhs)]
+        depth = zls * zhs
+        z = zh * zls + zl
+        z_up, z_down = shift(z, 1, depth), shift(z, -1, depth)
+        above = at(zl_=lax.rem(z_up, zls), zh_=z_up // zls)
+        below = at(zl_=lax.rem(z_down, zls), zh_=z_down // zls)
+        peers = [left, right, above, below]
         peers += [at(y_=shift(y, o, ys)) for o in range(1, ys)]
         peers += [x_peer(o, c) for o, c in x_peers]
-        peers += [at(zl_=shift(zl, o, zls)) for o in range(1, zls)]
         for peer in peers:
             pl.semaphore_signal(barrier, inc=1, device_id=peer, device_id_type=pl.DeviceIdType.MESH)
+
+        def give_tokens():
+            for sem, device in ((token_up, above), (token_down, below)):
+                pl.semaphore_signal(sem, inc=1, device_id=device, device_id_type=pl.DeviceIdType.MESH)
+
+        def token_round(index):
+            pl.semaphore_wait(token_up, 1)
+            pl.semaphore_wait(token_down, 1)
+            if index < ROUNDS - 1:
+                give_tokens()
 
         bufs = [buf_a, buf_b]
 
@@ -160,10 +176,16 @@
                 results.append(total)
             return results
 
-        def send_halo(s, c):
-            return [
-                send(sbuf.at[s, c, pl.ds(0, 7)], from_right.at[s, c], halo_send.at[s, c, 0], halo_recv.at[s, c, 0], left),
-                send(sbuf.at[s, c, pl.ds(1, 7)], from_left.at[s, c], halo_send.at[s, c, 1], halo_recv.at[s, c, 1], right),
+        halos = {}
+
+        def send_halo(s, c, h):
+            lanes = pl.ds(h * PIECE, PIECE)
+            halos[s, c, h] = [
+                send(
+                    sbuf.at[s, c, pl.ds(start, 7), :, lanes], into.at[s, c, :, :, lanes],
+                    halo_send.at[s, c, h, side], halo_recv.at[s, c, h, side], device,
+                )
+                for side, (start, into, device) in enumerate(((0, from_right, left), (1, from_left, right)))
             ]
 
         for c in range(CHUNKS):
@@ -172,15 +194,15 @@
                 lanes = pl.ds(q * LANES, LANES)
                 for p in range(PLANES):
                     split_store(0, c, p, lanes, buf_a[c, p, :, lanes])
+        pl.semaphore_wait(barrier, len(peers))
+        for c in range(CHUNKS):
+            for h in range(PIECES):
+                send_halo(0, c, h)
+        give_tokens()
         pot_load.wait()
         diag[...] = pot[...] + (3.0 * KINETIC * COEFFS[0] - CENTER)
         sten_load.wait()
-        local_part(0, 0)
-        pl.semaphore_wait(barrier, len(peers))
-        halos = {}
-        for c in range(CHUNKS):
-            halos[0, c] = send_halo(0, c)
-        for c in range(1, CHUNKS):
+        for c in range(CHUNKS):
             local_part(0, c)
 
         zh_up, zh_down, zh_far = shift(zh, 1, zhs), shift(zh, -1, zhs), shift(zh, 2, zhs)
@@ -199,21 +221,27 @@
                 sends.append(copy)
                 y_arrivals.append(copy)
 
+        rounds = 0
         for s in range(4):
             last = s == 3
             for c in range(CHUNKS):
-                for copy in halos[s, c]:
-                    copy.wait_recv()
-                for q in range(CELLS // LANES):
-                    lanes = pl.ds(q * LANES, LANES)
-                    results = finish(s, c, lanes)
-                    for p, value in enumerate(results):
-                        if last:
-                            rounded[c, q, p // 2, :, pl.ds((p % 2) * LANES, LANES)] = value.astype(jnp.bfloat16)
-                        else:
-                            split_store(s + 1, c, p, lanes, value)
+                for h in range(PIECES):
+                    for copy in halos[s, c, h]:
+                        copy.wait_recv()
+                    for q in range(h * PIECE // LANES, (h + 1) * PIECE // LANES):
+                        lanes = pl.ds(q * LANES, LANES)
+                        results = finish(s, c, lanes)
+                        for p, value in enumerate(results):
+                            if last:
+                                rounded[c, q, p // 2, :, pl.ds((p % 2) * LANES, LANES)] = value.astype(jnp.bfloat16)
+                            else:
+                                split_store(s + 1, c, p, lanes, value)
+                    if not last:
+                        send_halo(s + 1, c, h)
+                    if rounds < ROUNDS and (h == PIECES - 1 or (s, c) == (0, 0)):
+                        token_round(rounds)
+                        rounds += 1
                 if not last:
-                    halos[s + 1, c] = send_halo(s + 1, c)
                     local_part(s + 1, c)
                     continue
                 first, other = (zh_up, zh_down) if c == 0 else (zh_down, zh_up)
@@ -299,10 +327,8 @@
             mine = jnp.where(zh == o, total[:, o * width : (o + 1) * width], mine)
         corr_ref[...] = mine * (1.0 / (NZ * CELLS))
 
-        for s in range(4):
-            for c in range(CHUNKS):
-                for copy in halos[s, c]:
-                    copy.wait_send()
+        for copy in [one for pair in halos.values() for one in pair]:
+            copy.wait_send()
         for copy in list(relays.values()) + list(arrivals.values()) + sends:
             copy.wait_send()
         for copy in stores:
@@ -353,8 +379,10 @@
                 pltpu.VMEM((zhs, 8, LANES), f32),
                 dma((4,)),
                 dma((CHUNKS,)),
-                dma((4, CHUNKS, 2)),
-                dma((4, CHUNKS, 2)),
+                pltpu.SemaphoreType.REGULAR,
+                pltpu.SemaphoreType.REGULAR,
+                dma((4, CHUNKS, PIECES, 2)),
+                dma((4, CHUNKS, PIECES, 2)),
                 dma((CHUNKS, 3)),
                 dma((CHUNKS, 3)),
                 dma((CHUNKS,)),
@@ -369,7 +397,7 @@
                 dma((zhs,)),
             ],
             compiler_params=pltpu.CompilerParams(
-                collective_id=0, has_side_effects=True, vmem_limit_bytes=40 * 1024 * 1024
+                collective_id=0, has_side_effects=True, vmem_limit_bytes=60 * 1024 * 1024
             ),
             cost_estimate=pl.CostEstimate(flops=10**9, bytes_accessed=1500000, transcendentals=0),
         )(planes, potential, jnp.asarray(stencil))

time: 123 us -> 107 us (0.87)
  Pallas kernels: 118 us -> 104 us
  local copies, waits for them, and re-layouts: 4.09 us -> 2.37 us
    pallas_call x1, Pallas kernels: 118 us -> 104 us  [shards(): pl.pallas_call(make_kernel(xs, zls, ys, zhs), out_shape=(jax.ShapeDtypeSt...]
    unnamed x8 -> x4, local copies, waits for them, and re-layouts: 4.09 us -> 2.37 us
where the time goes in v2:
time: 107 us
  Pallas kernels  104 us (97%)
  local copies, waits for them, and re-layouts  2.37 us (2%)
    pallas_call x1, Pallas kernels, shards(): pl.pallas_call(make_kernel(xs, zls, ys, zhs), out_shape=(jax.ShapeDtypeSt...  104 us
    unnamed x4, local copies, waits for them, and re-layouts  2.37 us

profile of v2, /device:TPU:1, one launch (start us, length us, event | category | flops | bytes accessed | tf_op | source)
XLA Modules:
  0.0 106.6 jit_solution(5662386366053822355)
XLA Ops:
  0.6 103.6 %shard_map.50 = (f32[6,32,512]{2,1,0:T(8,128)}, f32[8,32]{1,0:T(8,128)}) custom-call(f32[6,32,512]{2,1,0:T(8,128)} %bitcast.5, f32[6,512]{1,0:T(8,128)} %pot_hbm.1, bf16[512,512]{1,0:T(8,128)(2,1)} %constant.2.clone.sten_hbm), custom_call_target="tpu_custom_call" | custom-call | flops 1000000000 | bytes 1500000 | tf_op jit(solution)/shard_map/pallas_call | solution.py:351
  104.3 0.0 copy-start
  104.3 1.8 %copy.7 = f32[32,6,512]{2,0,1:T(8,128)} copy(f32[32,6,512]{2,0,1:T(8,128)} %bitcast.3) | data formatting | bytes 786432
  106.0 0.0 copy-done
  106.1 0.6 copy.8
Async XLA Ops:
  104.3 1.8 %copy-start = (f32[8,32]{1,0:T(8,128)S(1)}, f32[8,32]{1,0:T(8,128)}, u32[]{:S(2)}) copy-start(f32[8,32]{1,0:T(8,128)} %get-tuple-element.5) | copy-start | bytes 3076

commit v3 on v2

--- a/solution.py
+++ b/solution.py
@@ -19,6 +19,7 @@
 PIECES = 2
 PIECE = CELLS // PIECES
 ROUNDS = 7
+RELAY = True
 
 COEFFS = [
     -5369.0 / 1800.0,
@@ -56,9 +57,9 @@
     def kernel(
         v_hbm, pot_hbm, sten_hbm, out_hbm, corr_ref,
         buf_a, buf_b, sten, pot, diag, sbuf, from_left, from_right,
-        rounded, relay, gathered, parts, got_x, sum_x, got_zl, sum_zl, got_zh,
+        rounded, relay, gathered, parts, got_x, packed, got_z,
         load_sem, store_sem, token_up, token_down, halo_send, halo_recv, z_send, z_recv, relay_recv, relay_send,
-        y_send, y_recv, x_send, x_recv, zl_send, zl_recv, zh_send, zh_recv,
+        y_send, y_recv, x_send, x_recv, d_send, d_recv,
     ):
         dom = lax.axis_index("dom")
         grp = lax.axis_index("grp")
@@ -172,7 +173,7 @@
                     total += couple[p + 6 - i] * lower[i]
                 for i in range(p + 1):
                     total += couple[6 + i - p] * upper[i]
-                nxt[c, p, :, lanes] = total
+                nxt[c, p, :, lanes] = total * 0.5 if s == 3 else total
                 results.append(total)
             return results
 
@@ -245,7 +246,10 @@
                     local_part(s + 1, c)
                     continue
                 first, other = (zh_up, zh_down) if c == 0 else (zh_down, zh_up)
-                relays[c] = send(rounded.at[c, zh_far], relay.at[c], z_send.at[c, 2], relay_recv.at[c], at(zh_=first))
+                if RELAY:
+                    relays[c] = send(rounded.at[c, zh_far], relay.at[c], z_send.at[c, 2], relay_recv.at[c], at(zh_=first))
+                else:
+                    arrivals[c, 2] = send(rounded.at[c, zh_far], gathered.at[y, zh, c], z_send.at[c, 2], z_recv.at[c, 2], at(zh_=zh_far))
                 arrivals[c, 0] = send(rounded.at[c, first], gathered.at[y, zh, c], z_send.at[c, 0], z_recv.at[c, 0], at(zh_=first))
                 arrivals[c, 1] = send(rounded.at[c, other], gathered.at[y, zh, c], z_send.at[c, 1], z_recv.at[c, 1], at(zh_=other))
                 gathered[y, zh, c] = rounded[c, zh]
@@ -258,8 +262,11 @@
 
         for c in range(CHUNKS):
             first, other = (zh_up, zh_down) if c == 0 else (zh_down, zh_up)
-            relays[c].wait_recv()
-            arrivals[c, 2] = send(relay.at[c], gathered.at[y, other, c], relay_send.at[c], z_recv.at[c, 2], at(zh_=first))
+            if RELAY:
+                relays[c].wait_recv()
+                arrivals[c, 2] = send(relay.at[c], gathered.at[y, other, c], relay_send.at[c], z_recv.at[c, 2], at(zh_=first))
+        for c in range(CHUNKS):
+            first, other = (zh_up, zh_down) if c == 0 else (zh_down, zh_up)
             arrivals[c, 0].wait_recv()
             spread_y(c, 1, other)
             arrivals[c, 1].wait_recv()
@@ -284,7 +291,7 @@
                 )
             total = total.reshape(zls, CORES, 8, own_rows)
             for b in range(CORES):
-                parts[off, b] = total[:, b]
+                parts[off, b] = total[:, b].reshape(zls // 2, 16, own_rows).astype(jnp.bfloat16)
             for flip in range(CORES):
                 if (off, flip) == (0, 0):
                     continue
@@ -294,38 +301,41 @@
                 )
                 sends.append(copy)
                 x_arrivals.append((off, flip, copy))
-        total = parts[0, core]
+        total = parts[0, core].astype(jnp.float32)
         for off, flip, copy in x_arrivals:
             copy.wait_recv()
-            total += got_x[off, flip]
-        sum_x[...] = total
-
-        zl_arrivals = []
-        for o in range(1, zls):
-            dest = shift(zl, o, zls)
-            copy = send(sum_x.at[dest], got_zl.at[o], zl_send.at[o], zl_recv.at[o], at(zl_=dest))
+            total += got_x[off, flip].astype(jnp.float32)
+        total = total.reshape(zls, 8, LANES)
+
+        width = CHUNKS * ROWS
+        row = lax.broadcasted_iota(jnp.int32, (8, LANES), 0) % 4
+        block = lax.broadcasted_iota(jnp.int32, (8, LANES), 1) // width
+        for l in range(zls):
+            turned = [total[l]] + [pltpu.roll(total[l], k * width, 1) for k in range(1, 4)]
+            for h in range(zhs):
+                mixed = jnp.zeros((8, LANES), jnp.float32)
+                for b in range(4):
+                    mixed = jnp.where((row == b) & (block == b), turned[(b - h) % 4], mixed)
+                mixed = mixed + pltpu.roll(mixed, 7, 0)
+                mixed = mixed + pltpu.roll(mixed, 6, 0)
+                packed[h * zls + l, pl.ds(0, 1)] = mixed[0:1]
+                packed[h * zls + l, pl.ds(1, 1)] = mixed[4:5]
+        d_arrivals = []
+        for o in sorted(range(1, depth), key=lambda o: -min(o, depth - o)):
+            dest = shift(z, o, depth)
+            copy = send(
+                packed.at[dest], got_z.at[o], d_send.at[o], d_recv.at[o],
+                at(zl_=lax.rem(dest, zls), zh_=dest // zls),
+            )
             sends.append(copy)
-            zl_arrivals.append(copy)
-        total = sum_x[zl]
-        for o, copy in enumerate(zl_arrivals):
+            d_arrivals.append((o, copy))
+        total = packed[z]
+        for o, copy in reversed(d_arrivals):
             copy.wait_recv()
-            total += got_zl[o + 1]
-        sum_zl[...] = total
-
-        zh_arrivals = []
-        for o in range(1, zhs):
-            dest = shift(zh, o, zhs)
-            copy = send(sum_zl, got_zh.at[o], zh_send.at[o], zh_recv.at[o], at(zh_=dest))
-            sends.append(copy)
-            zh_arrivals.append(copy)
-        for o, copy in enumerate(zh_arrivals):
-            copy.wait_recv()
-            total += got_zh[o + 1]
-        width = CHUNKS * ROWS
-        mine = jnp.zeros((8, width), jnp.float32)
-        for o in range(zhs):
-            mine = jnp.where(zh == o, total[:, o * width : (o + 1) * width], mine)
-        corr_ref[...] = mine * (1.0 / (NZ * CELLS))
+            total += got_z[o]
+        for a in range(2):
+            for b in range(4):
+                corr_ref[pl.ds(4 * a + b, 1), :] = total[a : a + 1, b * width : (b + 1) * width]
 
         for copy in [one for pair in halos.values() for one in pair]:
             copy.wait_send()
@@ -371,12 +381,10 @@
                 pltpu.VMEM((CHUNKS, zhs, 3, ROWS, 2 * LANES), bf16),
                 pltpu.VMEM((CHUNKS, 3, ROWS, 2 * LANES), bf16),
                 pltpu.VMEM((ys, zhs, CHUNKS, 3, ROWS, 2 * LANES), bf16),
-                pltpu.VMEM((xs, CORES, zls, 8, LANES), f32),
-                pltpu.VMEM((xs, CORES, zls, 8, LANES), f32),
-                pltpu.VMEM((zls, 8, LANES), f32),
-                pltpu.VMEM((zls, 8, LANES), f32),
-                pltpu.VMEM((8, LANES), f32),
-                pltpu.VMEM((zhs, 8, LANES), f32),
+                pltpu.VMEM((xs, CORES, zls // 2, 16, LANES), bf16),
+                pltpu.VMEM((xs, CORES, zls // 2, 16, LANES), bf16),
+                pltpu.VMEM((zls * zhs, 2, LANES), f32),
+                pltpu.VMEM((zls * zhs, 2, LANES), f32),
                 dma((4,)),
                 dma((CHUNKS,)),
                 pltpu.SemaphoreType.REGULAR,
@@ -391,17 +399,15 @@
                 dma((CHUNKS, 4, 3)),
                 dma((xs, CORES)),
                 dma((xs, CORES)),
-                dma((zls,)),
-                dma((zls,)),
-                dma((zhs,)),
-                dma((zhs,)),
+                dma((zls * zhs,)),
+                dma((zls * zhs,)),
             ],
             compiler_params=pltpu.CompilerParams(
                 collective_id=0, has_side_effects=True, vmem_limit_bytes=60 * 1024 * 1024
             ),
             cost_estimate=pl.CostEstimate(flops=10**9, bytes_accessed=1500000, transcendentals=0),
         )(planes, potential, jnp.asarray(stencil))
-        return jnp.transpose(filtered, (1, 0, 2)), jnp.transpose(corr, (1, 0))
+        return jnp.transpose(2.0 * filtered, (1, 0, 2)), jnp.transpose(corr, (1, 0)) * (1.0 / (NZ * CELLS))
 
     in_specs = (P("grp", "dom", None), P("dom", None))
     out_specs = (P("grp", "dom", None), P("grp", "dom"))

time: 107 us -> 101 us (0.944)
  Pallas kernels: 104 us -> 97.1 us
  other arithmetic: 0 us -> 2.38 us
  local copies, waits for them, and re-layouts: 2.37 us -> 0.01 us
    pallas_call x1, Pallas kernels: 104 us -> 97.1 us  [shards(): pl.pallas_call(make_kernel(xs, zls, ys, zhs), out_shape=(jax.ShapeDtypeSt...]
    unnamed x4 -> x2, local copies, waits for them, and re-layouts: 2.37 us -> 0.01 us
    transpose x0 -> x1, other arithmetic: none -> 1.78 us  [shards(): jnp.transpose(2.0 * filtered, (1, 0, 2))]
where the time goes in v3:
time: 101 us; the launch traced here: 100 us
  Pallas kernels  97.1 us (96%)
  other arithmetic  2.38 us (2%)
    pallas_call x1, Pallas kernels, shards(): pl.pallas_call(make_kernel(xs, zls, ys, zhs), out_shape=(jax.ShapeDtypeSt...  97.1 us

profile of v3, /device:TPU:1, one launch (start us, length us, event | category | flops | bytes accessed | tf_op | source)
XLA Modules:
  0.0 100.1 jit_solution(2734501458575271038)
XLA Ops:
  0.6 97.1 %shard_map.50 = (f32[6,32,512]{2,1,0:T(8,128)}, f32[8,32]{1,0:T(8,128)}) custom-call(f32[6,32,512]{2,1,0:T(8,128)} %bitcast.5, f32[6,512]{1,0:T(8,128)} %pot_hbm.1, bf16[512,512]{1,0:T(8,128)(2,1)} %constant.6.clone.sten_hbm), custom_call_target="tpu_custom_call" | custom-call | flops 1000000000 | bytes 1500000 | tf_op jit(solution)/shard_map/pallas_call | solution.py:361
  97.7 0.0 copy-start
  97.7 1.8 %multiply_bitcast_fusion = f32[32,6,512]{2,0,1:T(8,128)} fusion(f32[6,32,512]{2,1,0:T(8,128)} %get-tuple-element.4), kind=kLoop, calls=%fused_computation | loop fusion | flops 98304 | bytes 786432 | tf_op jit(solution)/shard_map/transpose | solution.py:410
  99.5 0.0 copy-done
  99.5 0.6 multiply_bitcast_fusion.1
Async XLA Ops:
  97.7 1.8 %copy-start = (f32[8,32]{1,0:T(8,128)S(1)}, f32[8,32]{1,0:T(8,128)}, u32[]{:S(2)}) copy-start(f32[8,32]{1,0:T(8,128)} %get-tuple-element.5) | copy-start | bytes 3076

commit v4 on v3

--- a/solution.py
+++ b/solution.py
@@ -19,7 +19,6 @@
 PIECES = 2
 PIECE = CELLS // PIECES
 ROUNDS = 7
-RELAY = True
 
 COEFFS = [
     -5369.0 / 1800.0,
@@ -195,8 +194,8 @@
                 lanes = pl.ds(q * LANES, LANES)
                 for p in range(PLANES):
                     split_store(0, c, p, lanes, buf_a[c, p, :, lanes])
-        pl.semaphore_wait(barrier, len(peers))
-        for c in range(CHUNKS):
+            if c == 0:
+                pl.semaphore_wait(barrier, len(peers))
             for h in range(PIECES):
                 send_halo(0, c, h)
         give_tokens()
@@ -246,12 +245,7 @@
                     local_part(s + 1, c)
                     continue
                 first, other = (zh_up, zh_down) if c == 0 else (zh_down, zh_up)
-                if RELAY:
-                    relays[c] = send(rounded.at[c, zh_far], relay.at[c], z_send.at[c, 2], relay_recv.at[c], at(zh_=first))
-                else:
-                    arrivals[c, 2] = send(rounded.at[c, zh_far], gathered.at[y, zh, c], z_send.at[c, 2], z_recv.at[c, 2], at(zh_=zh_far))
-                arrivals[c, 0] = send(rounded.at[c, first], gathered.at[y, zh, c], z_send.at[c, 0], z_recv.at[c, 0], at(zh_=first))
-                arrivals[c, 1] = send(rounded.at[c, other], gathered.at[y, zh, c], z_send.at[c, 1], z_recv.at[c, 1], at(zh_=other))
+                relays[c] = send(rounded.at[c, zh_far], relay.at[c], z_send.at[c, 2], relay_recv.at[c], at(zh_=first))
                 gathered[y, zh, c] = rounded[c, zh]
                 spread_y(c, 0, zh)
                 copy = pltpu.make_async_copy(
@@ -262,9 +256,13 @@
 
         for c in range(CHUNKS):
             first, other = (zh_up, zh_down) if c == 0 else (zh_down, zh_up)
-            if RELAY:
-                relays[c].wait_recv()
-                arrivals[c, 2] = send(relay.at[c], gathered.at[y, other, c], relay_send.at[c], z_recv.at[c, 2], at(zh_=first))
+            relays[c].wait_send()
+            arrivals[c, 0] = send(rounded.at[c, first], gathered.at[y, zh, c], z_send.at[c, 0], z_recv.at[c, 0], at(zh_=first))
+            arrivals[c, 1] = send(rounded.at[c, other], gathered.at[y, zh, c], z_send.at[c, 1], z_recv.at[c, 1], at(zh_=other))
+        for c in range(CHUNKS):
+            first, other = (zh_up, zh_down) if c == 0 else (zh_down, zh_up)
+            relays[c].wait_recv()
+            arrivals[c, 2] = send(relay.at[c], gathered.at[y, other, c], relay_send.at[c], z_recv.at[c, 2], at(zh_=first))
         for c in range(CHUNKS):
             first, other = (zh_up, zh_down) if c == 0 else (zh_down, zh_up)
             arrivals[c, 0].wait_recv()
@@ -339,7 +337,7 @@
 
         for copy in [one for pair in halos.values() for one in pair]:
             copy.wait_send()
-        for copy in list(relays.values()) + list(arrivals.values()) + sends:
+        for copy in list(arrivals.values()) + sends:
             copy.wait_send()
         for copy in stores:
             copy.wait()

time: 101 us -> 100 us (0.990)
  no operation moved by 1% of the time
where the time goes in v4:
time: 100 us
  Pallas kernels  97 us (97%)
  other arithmetic  2.38 us (2%)
    pallas_call x1, Pallas kernels, shards(): pl.pallas_call(make_kernel(xs, zls, ys, zhs), out_shape=(jax.ShapeDtypeSt...  97 us

profile of v4, /device:TPU:1, one launch (start us, length us, event | category | flops | bytes accessed | tf_op | source)
XLA Modules:
  0.0 100.1 jit_solution(12532441848811564942)
XLA Ops:
  0.6 97.0 %shard_map.50 = (f32[6,32,512]{2,1,0:T(8,128)}, f32[8,32]{1,0:T(8,128)}) custom-call(f32[6,32,512]{2,1,0:T(8,128)} %bitcast.5, f32[6,512]{1,0:T(8,128)} %pot_hbm.1, bf16[512,512]{1,0:T(8,128)(2,1)} %constant.6.clone.sten_hbm), custom_call_target="tpu_custom_call" | custom-call | flops 1000000000 | bytes 1500000 | tf_op jit(solution)/shard_map/pallas_call | solution.py:359
  97.7 0.0 copy-start
  97.7 1.8 %multiply_bitcast_fusion = f32[32,6,512]{2,0,1:T(8,128)} fusion(f32[6,32,512]{2,1,0:T(8,128)} %get-tuple-element.4), kind=kLoop, calls=%fused_computation | loop fusion | flops 98304 | bytes 786432 | tf_op jit(solution)/shard_map/transpose | solution.py:408
  99.5 0.0 copy-done
  99.5 0.6 multiply_bitcast_fusion.1
Async XLA Ops:
  97.7 1.8 %copy-start = (f32[8,32]{1,0:T(8,128)S(1)}, f32[8,32]{1,0:T(8,128)}, u32[]{:S(2)}) copy-start(f32[8,32]{1,0:T(8,128)} %get-tuple-element.5) | copy-start | bytes 3076
